TPU v7x, 512 devices: a whole 4x4x16 slice. The times are simulated.
512 devices in a mesh: gossip: 64 (over z, y_hi, core), tensor: 8 (over x, y_lo).
Axes of the slice: x: 4, y: 4 (y_hi: 2, y_lo: 2; y = y_hi * 2 + y_lo), z: 16, core: 2. Of those that a mesh axis runs over, the one named last changes fastest.
Arguments:
- inputs: bfloat16 [2, 2048, 20480], P(None, 'tensor', 'gossip'), may hold values from -6 to 6
- cotangent: bfloat16 [2, 2048, 20480], P(None, 'tensor', 'gossip'), may hold values from -6 to 6
- numerators: bfloat16 [64, 2048, 2048], P('gossip', None, 'tensor'), may hold values from -6 to 6
- momentum: bfloat16 [64, 2048, 2048], P('gossip', None, 'tensor'), may hold values from -6 to 6
- push_weight: float32 [64], P('gossip'), may hold values from 0.5 to 2
- step_index: int32 [], replicated, may hold values from 0 to 999
Outputs:
- numerators_out: bfloat16 [64, 2048, 2048], P('gossip', None, 'tensor')
- momentum_out: bfloat16 [64, 2048, 2048], P('gossip', None, 'tensor')
- weight_out: float32 [64], P('gossip')
- input_grads: bfloat16 [2, 2048, 20480], P(None, 'tensor', 'gossip')
All inputs are finite; a program needn't handle non-finite values.
Results may differ from a plain program's by a relative error of at most 0.02.
Values may be sent and summed in bfloat16 or wider, within the bound.
No kernel may reach another device: no remote copies, remote signals or barrier semaphores. Data moves between devices by JAX's collectives and lax.ppermute only.
A program may use at most 64 MiB of HBM per device.

v0:
```python
from functools import partial

import jax
import jax.numpy as jnp
from jax import lax
from jax.experimental import pallas as pl
from jax.experimental.pallas import tpu as pltpu
from jax.sharding import PartitionSpec as P

HEAD_DIM = 128
LEVELS = 6
PAD = 16
VMEM_LIMIT = 16 * 1024 * 1024
BF16 = jnp.bfloat16
VMEM = pl.BlockSpec(memory_space=pltpu.VMEM)
SMEM = pl.BlockSpec(memory_space=pltpu.SMEM)

CUTS = {
    "plain": lambda k: ((2048, (k,)),),
    "hops": lambda k: ((512, (4,) * (k // 4)),) * 4,
    "both": lambda k: ((1536, (k,)), (512, (-24, -24))),
}
LEVEL_PLANS = (
    ("plain", "plain", "apart", False),
    ("plain", "plain", "apart", True),
    ("plain", "plain", "late", False),
    ("hops", "both", "joined", False),
    ("hops", "plain", "joined", False),
    ("plain", "plain", "joined", False),
)


def passed_along(block, distance):
    count = lax.axis_size("gossip")
    route = [(i, (i + distance) % count) for i in range(count)]
    return lax.ppermute(block, "gossip", route)


def swapped_pair(block):
    count = lax.axis_size("tensor")
    return lax.ppermute(block, "tensor", [(i, i ^ 1) for i in range(count)])


def along_x(blocks):
    count = lax.axis_size("tensor")
    groups = [list(range(y, count, 2)) for y in range(2)]
    return lax.all_to_all(blocks, "tensor", 0, 0, axis_index_groups=groups)


def exchange(half, plan):
    parts, at = [], 0
    for number, (size, _) in enumerate(plan):
        size += PAD if number == len(plan) - 1 else 0
        parts.append(half if len(plan) == 1 else half[at : at + size])
        at += size
    for leg in range(max(len(legs) for _, legs in plan)):
        parts = [
            passed_along(part, legs[leg]) if leg < len(legs) else part
            for part, (_, legs) in zip(parts, plan)
        ]
    return parts


def call(kernel, out_shape, operands, name, cost=(0, 1 << 20), in_specs=None, out_specs=None, scratch=()):
    return pl.pallas_call(
        kernel,
        out_shape=out_shape,
        in_specs=in_specs or [VMEM] * len(operands),
        out_specs=out_specs or [VMEM] * len(out_shape),
        scratch_shapes=scratch,
        compiler_params=pltpu.CompilerParams(vmem_limit_bytes=VMEM_LIMIT),
        cost_estimate=pl.CostEstimate(flops=cost[0], bytes_accessed=cost[1], transcendentals=0),
        name=name,
    )(*operands)


def spread_kernel(inputs_ref, now_ref, later_ref):
    first = inputs_ref[0]
    for j in range(now_ref.shape[0]):
        now_ref[j, 0] = first
    later_ref[...] = inputs_ref[1]


def spread(inputs, count):
    _, tokens, width = inputs.shape
    many = jax.ShapeDtypeStruct((count, 1, tokens, width), BF16)
    one = jax.ShapeDtypeStruct((tokens, width), BF16)
    return call(spread_kernel, [many, one], [inputs], "spread")


def spread_pair_kernel(mine_ref, other_ref, spread_ref):
    here = lax.rem(lax.axis_index("tensor"), 2) == 0
    mine, other = mine_ref[...], other_ref[...]
    low = jnp.where(here, mine, other)
    high = jnp.where(here, other, mine)
    for x in range(spread_ref.shape[0]):
        spread_ref[x, 0] = low
        spread_ref[x, 1] = high


def spread_pair(mine, other, count):
    return call(
        spread_pair_kernel,
        [jax.ShapeDtypeStruct((count, 2, *mine.shape), BF16)],
        [mine, other],
        "spread_pair",
    )[0]


def head_backward(queries, upstream):
    results = []
    for start in range(0, queries.shape[1], HEAD_DIM):
        q = queries[:, start : start + HEAD_DIM]
        upper = upstream[:, start : start + HEAD_DIM].astype(jnp.float32)
        inverse = lax.rsqrt(jnp.mean(q * q, axis=1, keepdims=True) + 1e-06)
        normed = q * inverse
        inner = jnp.mean(upper * normed, axis=1, keepdims=True)
        results.append(inverse * (upper - normed * inner))
    return jnp.concatenate(results, axis=1)


def repeat(count, unroll, one):
    if unroll >= count:
        for j in range(count):
            one(j)
        return

    def several(turn, carry):
        for k in range(unroll):
            one(turn * unroll + k)
        return carry

    lax.fori_loop(0, count // unroll, several, 0)


def block_rows(j, block):
    return pl.ds(j * block if isinstance(j, int) else pl.multiple_of(j * block, block), block)


def step_kernel(
    factor, index, unroll, weight_ref, numer, features, upstream, momentum,
    half_out, momentum_out, debiased_out, grad_out, total,
):
    count, block = features.shape[0], features.shape[3]
    weight = jnp.full((1, block), weight_ref[0], jnp.float32)
    scale = 1.0 / weight
    total[...] = jnp.zeros_like(total)

    def query_term(j):
        rows = block_rows(j, block)
        divided = (numer[rows, :].astype(jnp.float32) * scale).astype(BF16)
        debiased_out[rows, :] = divided
        total[...] += jnp.dot(features[j, 0], divided, preferred_element_type=jnp.float32)

    repeat(count, unroll, query_term)
    grad = head_backward(factor * total[...], upstream[index]).astype(BF16)
    grad_out[...] = grad

    def update(j):
        rows = block_rows(j, block)
        grad_weight = factor * lax.dot_general(
            features[j, 0], grad_out[...], (((0,), (0,)), ((), ())), preferred_element_type=jnp.float32
        )
        moved = (0.9 * momentum[rows, :].astype(jnp.float32) + grad_weight).astype(BF16)
        momentum_out[rows, :] = moved
        held = numer[rows, :].astype(jnp.float32)
        half_out[rows, :] = (held - 0.25 * moved.astype(jnp.float32)).astype(BF16)

    repeat(count, unroll, update)
    high = weight.astype(BF16).astype(jnp.float32)
    line = lax.broadcasted_iota(jnp.int32, (PAD, block), 0)
    lines = jnp.where(line == 0, high, jnp.where(line == 1, weight - high, 0.0))
    half_out[pl.ds(count * block, PAD), :] = lines.astype(BF16)


def step(index, unroll, weight, numer, features, cotangent, momentum, factor):
    rows, width = momentum.shape
    tokens = cotangent.shape[1]
    operands = [weight, numer, features, cotangent, momentum]
    return call(
        partial(step_kernel, factor, index, unroll),
        [jax.ShapeDtypeStruct((n, width), BF16) for n in (rows + PAD, rows, rows, tokens)],
        operands,
        "optimizer_step",
        (4 * rows * width * tokens, 8 << 20),
        [SMEM] + [VMEM] * 4,
        scratch=[pltpu.VMEM((tokens, width), jnp.float32)],
    )


def average_kernel(sizes, own, *refs):
    came, numer, weight = refs[:-2], refs[-2], refs[-1]
    at, block = 0, 64
    for part, size in zip(came, sizes):

        def one(j, part=part, at=at):
            here = pl.ds(pl.multiple_of(at + j * block, block), block)
            both = own[here, :].astype(jnp.float32)
            both = both + part[pl.ds(pl.multiple_of(j * block, block), block), :].astype(jnp.float32)
            numer[here, :] = (both * 0.5).astype(BF16)

        repeat(size // block, 4, one)
        at += size
    mine = own[pl.ds(at, PAD), :].astype(jnp.float32)
    other = came[-1][pl.ds(sizes[-1], PAD), :].astype(jnp.float32)
    weight[0] = jnp.max((mine[0:1] + mine[1:2] + (other[0:1] + other[1:2])) * 0.5)


def average(own, came, plan):
    rows, width = own.shape[0] - PAD, own.shape[1]
    return call(
        partial(average_kernel, [size for size, _ in plan]),
        [jax.ShapeDtypeStruct((rows, width), BF16), jax.ShapeDtypeStruct((1,), jnp.float32)],
        [own, *came],
        "average",
        (1 << 50, 1 << 40),
        out_specs=[VMEM, SMEM],
    )


def blocks_kernel(factor, kept, *refs):
    out = refs[-1]
    count, block = out.shape[0], out.shape[3]
    for slot in range(kept):
        value = refs[slot][...]
        for j in range(count):
            out[j, slot] = value
    pairs = refs[kept:-1]

    def one(j):
        for number in range(len(pairs) // 2):
            debiased, grad = pairs[2 * number], pairs[2 * number + 1]
            part = lax.dot_general(
                grad[...],
                debiased[block_rows(j, block), :],
                (((1,), (1,)), ((), ())),
                preferred_element_type=jnp.float32,
            )
            out[j, kept + number] = (factor * part).astype(BF16)

    if pairs:
        repeat(count, 2, one)


def blocks_for_peers(factor, kept, pairs):
    tokens, width = (kept or pairs[0][1:])[0].shape
    count = lax.axis_size("tensor")
    operands = [*kept, *(ref for pair in pairs for ref in pair)]
    return call(
        partial(blocks_kernel, factor, len(kept)),
        [jax.ShapeDtypeStruct((count, len(kept) + len(pairs), tokens, width), BF16)],
        operands,
        "blocks_for_peers",
        (2 * len(pairs) * count * width * width * tokens, 3 << 20),
    )[0]


def total_of(ref, places):
    total = None
    for place in places:
        term = ref[place].astype(jnp.float32)
        total = term if total is None else total + term
    return total


def add_kernel(mine_ref, came_ref, out_ref):
    out_ref[...] = (mine_ref[...] + came_ref[...].astype(jnp.float32)).astype(BF16)


def pair_kernel(in_ref, mine_ref, other_ref):
    count = in_ref.shape[0]
    sums = [total_of(in_ref, [(x, y) for x in range(count)]) for y in range(2)]
    here = lax.rem(lax.axis_index("tensor"), 2) == 0
    mine_ref[...] = jnp.where(here, sums[0], sums[1])
    other_ref[...] = jnp.where(here, sums[1], sums[0]).astype(BF16)


def sum_kernel(slot, in_ref, out_ref):
    out_ref[...] = total_of(in_ref, [(j, slot) for j in range(in_ref.shape[0])]).astype(BF16)


def collect_kernel(slots, first_ref, second_ref, out_ref):
    for index, (slot, ref) in enumerate(zip(slots, (first_ref, second_ref))):
        if slot is None:
            out_ref[index] = ref[...]
        else:
            places = [(j, slot) for j in range(ref.shape[0])]
            out_ref[index] = total_of(ref, places).astype(BF16)


def swapped_all(blocks):
    return lax.all_to_all(blocks, "tensor", 0, 0)


def first_sum(swapped, kind):
    shape = swapped.shape[-2:]
    result = [jax.ShapeDtypeStruct(shape, BF16)]
    if kind == "joined":
        return call(partial(sum_kernel, 1), result, [swapped], "sum_terms")[0]
    mine, other = call(
        pair_kernel, [jax.ShapeDtypeStruct(shape, jnp.float32), *result], [swapped], "sum_pair"
    )
    return call(add_kernel, result, [mine, swapped_pair(other)], "add_pair")[0]


def after_first_half(level, factor, half, velocity, debiased, grad, later, cotangent):
    first, second, kind, x_gather = LEVEL_PLANS[level]
    first = CUTS[first](1 << level)
    second = CUTS[second](1 << ((level + 1) % LEVELS))
    shape, count = later.shape, lax.axis_size("tensor")
    came = exchange(half, first)
    if x_gather:
        pairs = spread_pair(later, swapped_pair(later), count // 2)
        features = along_x(pairs).reshape(count, 1, *shape)
    else:
        terms = [(debiased, grad)] if kind == "joined" else []
        features = swapped_all(blocks_for_peers(factor, [later], terms))
    if kind == "apart":
        terms = blocks_for_peers(factor, [], [(debiased, grad)])
        swapped = along_x(terms.reshape(count // 2, 2, *shape))
    else:
        swapped = features
    numer, weight = average(half, came, first)
    half, velocity, debiased_2, grad_2 = step(
        1, 4, weight, numer, features, cotangent, velocity, factor
    )
    came = exchange(half, second)
    terms = [(debiased_2, grad_2)]
    if kind == "late":
        terms.insert(0, (debiased, grad))
    else:
        grad_in = first_sum(swapped, kind)
    swapped = swapped_all(blocks_for_peers(factor, [], terms))
    numer, weight = average(half, came, second)
    swapped, numer = lax.optimization_barrier((swapped, numer))
    slots, parts = ((0, 1), [swapped] * 2) if kind == "late" else ((None, 0), [grad_in, swapped])
    grads = call(
        partial(collect_kernel, slots),
        [jax.ShapeDtypeStruct((2, *shape), BF16)],
        parts,
        "collect",
    )[0]
    return numer, velocity, weight, grads


def body(inputs, cotangent, numerators, momentum, push_weight, step_index):
    inputs, cotangent = inputs.transpose(0, 2, 1), cotangent.transpose(0, 2, 1)
    tensors = lax.axis_size("tensor")
    factor = (inputs.shape[2] * tensors) ** (-0.5)
    now, later = spread(inputs, tensors)
    half, velocity, debiased, grad = step(
        0, tensors, push_weight, numerators[0], swapped_all(now), cotangent, momentum[0], factor
    )
    numer, velocity, weight, grads = lax.switch(
        lax.rem(step_index, LEVELS),
        [partial(after_first_half, level, factor) for level in range(LEVELS)],
        half,
        velocity,
        debiased,
        grad,
        later,
        cotangent,
    )
    return numer[None], velocity[None], weight, grads.transpose(0, 2, 1)


def solution(mesh):
    placed = (
        P(None, "tensor", "gossip"),
        P(None, "tensor", "gossip"),
        P("gossip", None, "tensor"),
        P("gossip", None, "tensor"),
        P("gossip"),
        P(),
    )
    return jax.shard_map(
        body,
        mesh=mesh,
        in_specs=placed,
        out_specs=(
            P("gossip", None, "tensor"),
            P("gossip", None, "tensor"),
            P("gossip"),
            P(None, "tensor", "gossip"),
        ),
        check_vma=False,
    )
```

profile of v0, /device:TPU:16, one launch (start us, length us, event | category | flops | bytes accessed | tf_op | source)
XLA Modules:
  0.0 129.8 jit_solution(3958727850763477598)
XLA Ops:
  0.6 0.0 copy-start.2
  0.6 1.0 copy-done.2
  1.6 1.2 spread.1
  2.8 0.0 copy-start
  2.8 0.0 copy-start.1
  2.8 5.2 %all-to-all-start.14 = ((bf16[8,1,320,256]{3,2,1,0:T(8,128)(2,1)}), bf16[8,1,320,256]{3,2,1,0:T(8,128)(2,1)S(1)}, u32[]{:S(2)}, u32[]{:S(2)}) async-start(bf16[8,1,320,256]{3,2,1,0:T(8,128)(2,1)} %get-tuple-element.186), calls=%async_computation.14 | async-start | bytes 2621440 | tf_op jit(solution)/shard_map/all_to_all | solution.py:292
  9.3 18.6 %all-to-all-done.14.features = bf16[8,1,320,256]{3,2,1,0:T(8,128)(2,1)S(1)} async-done(((bf16[8,1,320,256]{3,2,1,0:T(8,128)(2,1)}), bf16[8,1,320,256]{3,2,1,0:T(8,128)(2,1)S(1)}, u32[]{:S(2)}, u32[]{:S(2)}) %all-to-all-start.14) | async-done | bytes 1310752 | tf_op jit(solution)/shard_map/all_to_all | solution.py:292
  27.9 0.0 copy-done
  27.9 0.0 copy-done.1
  27.9 0.0 copy-start.20
  27.9 4.7 %optimizer_step.13 = (bf16[2064,256]{1,0:T(8,128)(2,1)}, bf16[2048,256]{1,0:T(8,128)(2,1)}, bf16[2048,256]{1,0:T(8,128)(2,1)}, bf16[320,256]{1,0:T(8,128)(2,1)}) custom-call(f32[1]{0:T(128)S(6)} %copy.34.weight_ref, bf16[2048,256]{1,0:T(8,128)(2,1)S(1)} %bitcast.11, bf16[8,1,320,256]{3,2,1,0:T(8,128)(2,1)S(1)} %all-to-all-done.14.features, ...), custom_call_target="tpu_custom_call" | custom-call | flops 671088640 | bytes 8388608 | tf_op jit(solution)/shard_map/optimizer_step/pallas_call | solution.py:65
  32.6 0.0 copy-done.20
  32.6 97.2 %conditional.1 = (bf16[2048,256]{1,0:T(8,128)(2,1)}, bf16[2048,256]{1,0:T(8,128)(2,1)}, f32[1]{0:T(128)}, bf16[2,320,256]{2,1,0:T(8,128)(2,1)}) conditional(s32[]{:T(128)} %clamp.3, (bf16[2064,256]{1,0:T(8,128)(2,1)}, bf16[320,256]{1,0:T(8,128)(2,1)S(1)}, bf16[2,320,256]{2,1,0:T(8,128)(2,1)}, ...), branch_computations={%region_0.0_spmd, %region_1.0_spmd, %region_2.0_spmd, %region_3.0_... | conditional | flops 2251801155862528 | bytes 2199081189376 | solution.py:354
  32.6 3.8 %collective-permute-start.7 = (bf16[2064,256]{1,0:T(8,128)(2,1)}, bf16[2064,256]{1,0:T(8,128)(2,1)S(1)}, u32[]{:S(2)}, u32[]{:S(2)}) collective-permute-start(bf16[2064,256]{1,0:T(8,128)(2,1)} %get-tuple-element.110.own), channel_id=1, source_target_pairs={{0,32},{8,40},{16,48},{24,56},{32,64},{40,72},{48,80},{56,88},{64,... | collective-permute-start | bytes 3170312 | tf_op jit(solution)/shard_map/cond/branch_2_fun/ppermute | solution.py:36
  36.4 1.1 blocks_for_peers.18
  37.6 4.3 %all-to-all-start.6 = ((bf16[8,1,320,256]{3,2,1,0:T(8,128)(2,1)}), bf16[8,1,320,256]{3,2,1,0:T(8,128)(2,1)}, u32[]{:S(2)}, u32[]{:S(2)}) async-start(bf16[8,1,320,256]{3,2,1,0:T(8,128)(2,1)} %blocks_for_peers.18), calls=%async_computation.6 | async-start | bytes 2621440 | tf_op jit(solution)/shard_map/cond/branch_2_fun/all_to_all | solution.py:292
  41.9 24.7 %collective-permute-done.7.refs_0_ = bf16[2064,256]{1,0:T(8,128)(2,1)S(1)} collective-permute-done((bf16[2064,256]{1,0:T(8,128)(2,1)}, bf16[2064,256]{1,0:T(8,128)(2,1)S(1)}, u32[]{:S(2)}, u32[]{:S(2)}) %collective-permute-start.7) | collective-permute-done | bytes 1056800 | tf_op jit(solution)/shard_map/cond/branch_2_fun/ppermute | solution.py:36
  66.6 2.3 %average.16 = (bf16[2048,256]{1,0:T(8,128)(2,1)S(1)}, f32[1]{0:T(128)}) custom-call(bf16[2064,256]{1,0:T(8,128)(2,1)} %get-tuple-element.110.own, bf16[2064,256]{1,0:T(8,128)(2,1)S(1)} %collective-permute-done.7.refs_0_), custom_call_target="tpu_custom_call" | custom-call | flops 1125899906842624 | bytes 1099511627776 | tf_op jit(solution)/shard_map/cond/branch_2_fun/average/pallas_call | solution.py:65
  68.9 0.0 copy-start.5
  68.9 0.0 all-to-all-done.6.features
  68.9 0.0 copy-start.18
  68.9 0.0 copy-done.14
  68.9 5.6 %optimizer_step.9 = (bf16[2064,256]{1,0:T(8,128)(2,1)S(1)}, bf16[2048,256]{1,0:T(8,128)(2,1)}, bf16[2048,256]{1,0:T(8,128)(2,1)S(1)}, bf16[320,256]{1,0:T(8,128)(2,1)S(1)}) custom-call(f32[1]{0:T(128)} %get-tuple-element.111.weight_ref, bf16[2048,256]{1,0:T(8,128)(2,1)S(1)} %get-tuple-element.112.numer, bf16[8,1,320,256]{3,2,1,0:T(8,128)(2,1)} %all-to-all-done.6.features, ...), custom_call_target="tpu_custom_call" | custom-call | flops 671088640 | bytes 8388608 | tf_op jit(solution)/shard_map/cond/branch_2_fun/optimizer_step/pallas_call | solution.py:65
  74.5 1.9 %collective-permute-start.8 = (bf16[2064,256]{1,0:T(8,128)(2,1)S(1)}, bf16[2064,256]{1,0:T(8,128)(2,1)S(1)}, u32[]{:S(2)}, u32[]{:S(2)}) collective-permute-start(bf16[2064,256]{1,0:T(8,128)(2,1)S(1)} %get-tuple-element.118.own), channel_id=1, source_target_pairs={{0,64},{8,72},{16,80},{24,88},{32,96},{40,104},{48,112},{56,120},{... | collective-permute-start | bytes 3170312 | tf_op jit(solution)/shard_map/cond/branch_2_fun/ppermute | solution.py:36
  76.4 0.0 copy-done.5
  76.4 0.0 copy-done.18
  76.4 3.0 %blocks_for_peers.19 = bf16[8,2,320,256]{3,2,1,0:T(8,128)(2,1)} custom-call(bf16[2048,256]{1,0:T(8,128)(2,1)S(1)} %copy-done.5, bf16[320,256]{1,0:T(8,128)(2,1)S(1)} %copy-done.18, bf16[2048,256]{1,0:T(8,128)(2,1)S(1)} %get-tuple-element.116.refs_2_, bf16[320,256]{1,0:T(8,128)(2,1)S(1)} %get-tuple-element.117.refs_3_), custom_call_target="tpu_custom_call" | custom-call | flops 671088640 | bytes 3145728 | tf_op jit(solution)/shard_map/cond/branch_2_fun/blocks_for_peers/pallas_call | solution.py:65
  79.5 4.4 %all-to-all-start.7 = ((bf16[8,2,320,256]{3,2,1,0:T(8,128)(2,1)}), bf16[8,2,320,256]{3,2,1,0:T(8,128)(2,1)}, u32[]{:S(2)}, u32[]{:S(2)}) async-start(bf16[8,2,320,256]{3,2,1,0:T(8,128)(2,1)} %blocks_for_peers.19), calls=%async_computation.7 | async-start | bytes 5242880 | tf_op jit(solution)/shard_map/cond/branch_2_fun/all_to_all | solution.py:292
  83.9 40.9 %collective-permute-done.8.refs_0_ = bf16[2064,256]{1,0:T(8,128)(2,1)S(1)} collective-permute-done((bf16[2064,256]{1,0:T(8,128)(2,1)S(1)}, bf16[2064,256]{1,0:T(8,128)(2,1)S(1)}, u32[]{:S(2)}, u32[]{:S(2)}) %collective-permute-start.8) | collective-permute-done | bytes 1056800 | tf_op jit(solution)/shard_map/cond/branch_2_fun/ppermute | solution.py:36
  124.8 1.3 %average.17 = (bf16[2048,256]{1,0:T(8,128)(2,1)}, f32[1]{0:T(128)}) custom-call(bf16[2064,256]{1,0:T(8,128)(2,1)S(1)} %get-tuple-element.118.own, bf16[2064,256]{1,0:T(8,128)(2,1)S(1)} %collective-permute-done.8.refs_0_), custom_call_target="tpu_custom_call" | custom-call | flops 1125899906842624 | bytes 1099511627776 | tf_op jit(solution)/shard_map/cond/branch_2_fun/average/pallas_call | solution.py:65
  126.2 0.0 all-to-all-done.7.first_ref.second_ref
  126.2 3.6 %collect.8 = bf16[2,320,256]{2,1,0:T(8,128)(2,1)} custom-call(bf16[8,2,320,256]{3,2,1,0:T(8,128)(2,1)} %all-to-all-done.7.first_ref.second_ref, bf16[8,2,320,256]{3,2,1,0:T(8,128)(2,1)} %all-to-all-done.7.first_ref.second_ref), custom_call_target="tpu_custom_call" | custom-call | bytes 1048576 | tf_op jit(solution)/shard_map/cond/branch_2_fun/collect/pallas_call | solution.py:65
  (1 shorter events, 0.0 us)
Async XLA Ops:
  0.6 1.0 copy-start.2
  2.8 25.1 %copy-start = (bf16[1,2048,256]{2,1,0:T(8,128)(2,1)S(1)}, bf16[1,2048,256]{2,1,0:T(8,128)(2,1)}, u32[]{:S(2)}) copy-start(bf16[1,2048,256]{2,1,0:T(8,128)(2,1)} %param.14) | copy-start | bytes 3145732
  2.8 25.1 %copy-start.1 = (bf16[1,2048,256]{2,1,0:T(8,128)(2,1)S(1)}, bf16[1,2048,256]{2,1,0:T(8,128)(2,1)}, u32[]{:S(2)}) copy-start(bf16[1,2048,256]{2,1,0:T(8,128)(2,1)} %param.15) | copy-start | bytes 3145732
  2.8 25.1 %all-to-all-start.14 = ((bf16[8,1,320,256]{3,2,1,0:T(8,128)(2,1)}), bf16[8,1,320,256]{3,2,1,0:T(8,128)(2,1)S(1)}, u32[]{:S(2)}, u32[]{:S(2)}) async-start(bf16[8,1,320,256]{3,2,1,0:T(8,128)(2,1)} %get-tuple-element.186), calls=%async_computation.14 | async-start | bytes 2621440 | tf_op jit(solution)/shard_map/all_to_all | solution.py:292
  27.9 4.7 %copy-start.20 = (bf16[320,256]{1,0:T(8,128)(2,1)S(1)}, bf16[320,256]{1,0:T(8,128)(2,1)}, u32[]{:S(2)}) copy-start(bf16[320,256]{1,0:T(8,128)(2,1)} %get-tuple-element.188) | copy-start | bytes 491524
  32.6 34.0 %collective-permute-start.7 = (bf16[2064,256]{1,0:T(8,128)(2,1)}, bf16[2064,256]{1,0:T(8,128)(2,1)S(1)}, u32[]{:S(2)}, u32[]{:S(2)}) collective-permute-start(bf16[2064,256]{1,0:T(8,128)(2,1)} %get-tuple-element.110.own), channel_id=1, source_target_pairs={{0,32},{8,40},{16,48},{24,56},{32,64},{40,72},{48,80},{56,88},{64,... | collective-permute-start | bytes 3170312 | tf_op jit(solution)/shard_map/cond/branch_2_fun/ppermute | solution.py:36
  37.6 31.3 %all-to-all-start.6 = ((bf16[8,1,320,256]{3,2,1,0:T(8,128)(2,1)}), bf16[8,1,320,256]{3,2,1,0:T(8,128)(2,1)}, u32[]{:S(2)}, u32[]{:S(2)}) async-start(bf16[8,1,320,256]{3,2,1,0:T(8,128)(2,1)} %blocks_for_peers.18), calls=%async_computation.6 | async-start | bytes 2621440 | tf_op jit(solution)/shard_map/cond/branch_2_fun/all_to_all | solution.py:292
  66.6 2.3 %copy-start.14 = (bf16[2,320,256]{2,1,0:T(8,128)(2,1)S(1)}, bf16[2,320,256]{2,1,0:T(8,128)(2,1)}, u32[]{:S(2)}) copy-start(bf16[2,320,256]{2,1,0:T(8,128)(2,1)} %get-tuple-element.114.upstream) | copy-start | bytes 983044 | tf_op jit(solution)/shard_map/cond
  68.9 7.5 %copy-start.5 = (bf16[2048,256]{1,0:T(8,128)(2,1)S(1)}, bf16[2048,256]{1,0:T(8,128)(2,1)}, u32[]{:S(2)}) copy-start(bf16[2048,256]{1,0:T(8,128)(2,1)} %get-tuple-element.108.refs_0_) | copy-start | bytes 3145732 | tf_op jit(solution)/shard_map/cond
  68.9 7.5 %copy-start.18 = (bf16[320,256]{1,0:T(8,128)(2,1)S(1)}, bf16[320,256]{1,0:T(8,128)(2,1)}, u32[]{:S(2)}) copy-start(bf16[320,256]{1,0:T(8,128)(2,1)} %get-tuple-element.109.refs_1_) | copy-start | bytes 491524 | tf_op jit(solution)/shard_map/cond
  74.5 50.3 %collective-permute-start.8 = (bf16[2064,256]{1,0:T(8,128)(2,1)S(1)}, bf16[2064,256]{1,0:T(8,128)(2,1)S(1)}, u32[]{:S(2)}, u32[]{:S(2)}) collective-permute-start(bf16[2064,256]{1,0:T(8,128)(2,1)S(1)} %get-tuple-element.118.own), channel_id=1, source_target_pairs={{0,64},{8,72},{16,80},{24,88},{32,96},{40,104},{48,112},{56,120},{... | collective-permute-start | bytes 3170312 | tf_op jit(solution)/shard_map/cond/branch_2_fun/ppermute | solution.py:36
  79.5 46.7 %all-to-all-start.7 = ((bf16[8,2,320,256]{3,2,1,0:T(8,128)(2,1)}), bf16[8,2,320,256]{3,2,1,0:T(8,128)(2,1)}, u32[]{:S(2)}, u32[]{:S(2)}) async-start(bf16[8,2,320,256]{3,2,1,0:T(8,128)(2,1)} %blocks_for_peers.19), calls=%async_computation.7 | async-start | bytes 5242880 | tf_op jit(solution)/shard_map/cond/branch_2_fun/all_to_all | solution.py:292
where the time goes:
time: 130 us
  waiting for transfers between devices  84.2 us (65%)
  Pallas kernels  22.9 us (18%)
  starting transfers between devices  19.6 us (15%)
  between operations  1.95 us (2%)
    ppermute x2, waiting for transfers between devices, passed_along(): return lax.ppermute(block, 'gossip', route)  65.6 us
    pallas_call x8, Pallas kernels, call(): pl.pallas_call(kernel, out_shape=out_shape, in_specs=in_specs or [VMEM] *...  22.9 us
    all_to_all x3, waiting for transfers between devices, swapped_all(): return lax.all_to_all(blocks, 'tensor', 0, 0)  18.6 us
    all_to_all x3, starting transfers between devices, swapped_all(): return lax.all_to_all(blocks, 'tensor', 0, 0)  13.9 us
    ppermute x2, starting transfers between devices, passed_along(): return lax.ppermute(block, 'gossip', route)  5.72 us
  transfers between devices with their start and end apart: 5, of which 3 were waited for; matrix products, arithmetic and copies ran while one was open for 0% of the time, Pallas kernels for 6%

commit v1 on v0

--- a/solution.py
+++ b/solution.py
@@ -14,19 +14,20 @@
 BF16 = jnp.bfloat16
 VMEM = pl.BlockSpec(memory_space=pltpu.VMEM)
 SMEM = pl.BlockSpec(memory_space=pltpu.SMEM)
+HBM = pl.BlockSpec(memory_space=pltpu.HBM)
 
 CUTS = {
     "plain": lambda k: ((2048, (k,)),),
     "hops": lambda k: ((512, (4,) * (k // 4)),) * 4,
-    "both": lambda k: ((1536, (k,)), (512, (-24, -24))),
+    "both": lambda k: ((1664, (k,)), (384, (-24, -24))),
 }
 LEVEL_PLANS = (
-    ("plain", "plain", "apart", False),
-    ("plain", "plain", "apart", True),
-    ("plain", "plain", "late", False),
-    ("hops", "both", "joined", False),
-    ("hops", "plain", "joined", False),
-    ("plain", "plain", "joined", False),
+    ("plain", "plain", "late", False, True),
+    ("plain", "plain", "late", True, False),
+    ("plain", "plain", "late", False, False),
+    ("hops", "both", "late", False, False),
+    ("hops", "plain", "late", False, False),
+    ("plain", "plain", "joined", False, False),
 )
 
 
@@ -74,18 +75,25 @@
     )(*operands)
 
 
-def spread_kernel(inputs_ref, now_ref, later_ref):
-    first = inputs_ref[0]
+def spread_kernel(inputs_ref, now_ref, first, semaphore):
+    load = pltpu.make_async_copy(inputs_ref.at[0], first, semaphore)
+    load.start()
+    load.wait()
+    value = first[...]
     for j in range(now_ref.shape[0]):
-        now_ref[j, 0] = first
-    later_ref[...] = inputs_ref[1]
+        now_ref[j, 0] = value
 
 
 def spread(inputs, count):
-    _, tokens, width = inputs.shape
-    many = jax.ShapeDtypeStruct((count, 1, tokens, width), BF16)
-    one = jax.ShapeDtypeStruct((tokens, width), BF16)
-    return call(spread_kernel, [many, one], [inputs], "spread")
+    block = inputs.shape[1:]
+    return call(
+        spread_kernel,
+        [jax.ShapeDtypeStruct((count, 1, *block), BF16)],
+        [inputs],
+        "spread",
+        in_specs=[HBM],
+        scratch=[pltpu.VMEM(block, BF16), pltpu.SemaphoreType.DMA],
+    )[0]
 
 
 def spread_pair_kernel(mine_ref, other_ref, spread_ref):
@@ -199,21 +207,21 @@
             both = both + part[pl.ds(pl.multiple_of(j * block, block), block), :].astype(jnp.float32)
             numer[here, :] = (both * 0.5).astype(BF16)
 
-        repeat(size // block, 4, one)
+        repeat(size // block, 2, one)
         at += size
     mine = own[pl.ds(at, PAD), :].astype(jnp.float32)
     other = came[-1][pl.ds(sizes[-1], PAD), :].astype(jnp.float32)
     weight[0] = jnp.max((mine[0:1] + mine[1:2] + (other[0:1] + other[1:2])) * 0.5)
 
 
-def average(own, came, plan):
+def average(own, came, plan, cost):
     rows, width = own.shape[0] - PAD, own.shape[1]
     return call(
         partial(average_kernel, [size for size, _ in plan]),
         [jax.ShapeDtypeStruct((rows, width), BF16), jax.ShapeDtypeStruct((1,), jnp.float32)],
         [own, *came],
         "average",
-        (1 << 50, 1 << 40),
+        (1 << cost, 1 << 20),
         out_specs=[VMEM, SMEM],
     )
 
@@ -269,10 +277,11 @@
 
 def pair_kernel(in_ref, mine_ref, other_ref):
     count = in_ref.shape[0]
-    sums = [total_of(in_ref, [(x, y) for x in range(count)]) for y in range(2)]
     here = lax.rem(lax.axis_index("tensor"), 2) == 0
-    mine_ref[...] = jnp.where(here, sums[0], sums[1])
-    other_ref[...] = jnp.where(here, sums[1], sums[0]).astype(BF16)
+    for slot in range(in_ref.shape[2]):
+        low, high = (total_of(in_ref, [(x, y, slot) for x in range(count)]) for y in range(2))
+        mine_ref[slot] = jnp.where(here, low, high)
+        other_ref[slot] = jnp.where(here, high, low).astype(BF16)
 
 
 def sum_kernel(slot, in_ref, out_ref):
@@ -292,35 +301,21 @@
     return lax.all_to_all(blocks, "tensor", 0, 0)
 
 
-def first_sum(swapped, kind):
-    shape = swapped.shape[-2:]
-    result = [jax.ShapeDtypeStruct(shape, BF16)]
-    if kind == "joined":
-        return call(partial(sum_kernel, 1), result, [swapped], "sum_terms")[0]
-    mine, other = call(
-        pair_kernel, [jax.ShapeDtypeStruct(shape, jnp.float32), *result], [swapped], "sum_pair"
-    )
-    return call(add_kernel, result, [mine, swapped_pair(other)], "add_pair")[0]
-
-
 def after_first_half(level, factor, half, velocity, debiased, grad, later, cotangent):
-    first, second, kind, x_gather = LEVEL_PLANS[level]
+    first, second, kind, x_gather, x_sum = LEVEL_PLANS[level]
     first = CUTS[first](1 << level)
     second = CUTS[second](1 << ((level + 1) % LEVELS))
     shape, count = later.shape, lax.axis_size("tensor")
-    came = exchange(half, first)
+    one, both = jax.ShapeDtypeStruct(shape, BF16), jax.ShapeDtypeStruct((2, *shape), BF16)
     if x_gather:
-        pairs = spread_pair(later, swapped_pair(later), count // 2)
+        half, other = lax.optimization_barrier((half, swapped_pair(later)))
+        pairs = spread_pair(later, other, count // 2)
         features = along_x(pairs).reshape(count, 1, *shape)
     else:
         terms = [(debiased, grad)] if kind == "joined" else []
         features = swapped_all(blocks_for_peers(factor, [later], terms))
-    if kind == "apart":
-        terms = blocks_for_peers(factor, [], [(debiased, grad)])
-        swapped = along_x(terms.reshape(count // 2, 2, *shape))
-    else:
-        swapped = features
-    numer, weight = average(half, came, first)
+    came = exchange(half, first)
+    numer, weight = average(half, came, first, 35 if kind == "joined" else 33)
     half, velocity, debiased_2, grad_2 = step(
         1, 4, weight, numer, features, cotangent, velocity, factor
     )
@@ -329,17 +324,21 @@
     if kind == "late":
         terms.insert(0, (debiased, grad))
     else:
-        grad_in = first_sum(swapped, kind)
-    swapped = swapped_all(blocks_for_peers(factor, [], terms))
-    numer, weight = average(half, came, second)
+        grad_in = call(partial(sum_kernel, 1), [one], [features], "sum_terms")[0]
+    blocks = blocks_for_peers(factor, [], terms)
+    if x_sum:
+        swapped = along_x(blocks.reshape(count // 2, 2, *blocks.shape[1:]))
+    else:
+        swapped = swapped_all(blocks)
+    numer, weight = average(half, came, second, 35)
     swapped, numer = lax.optimization_barrier((swapped, numer))
-    slots, parts = ((0, 1), [swapped] * 2) if kind == "late" else ((None, 0), [grad_in, swapped])
-    grads = call(
-        partial(collect_kernel, slots),
-        [jax.ShapeDtypeStruct((2, *shape), BF16)],
-        parts,
-        "collect",
-    )[0]
+    if x_sum:
+        wide = jax.ShapeDtypeStruct(both.shape, jnp.float32)
+        mine, other = call(pair_kernel, [wide, both], [swapped], "sum_pair")
+        grads = call(add_kernel, [both], [mine, swapped_pair(other)], "add_pair")[0]
+    else:
+        slots, parts = ((0, 1), [swapped] * 2) if kind == "late" else ((None, 0), [grad_in, swapped])
+        grads = call(partial(collect_kernel, slots), [both], parts, "collect")[0]
     return numer, velocity, weight, grads
 
 
@@ -347,7 +346,7 @@
     inputs, cotangent = inputs.transpose(0, 2, 1), cotangent.transpose(0, 2, 1)
     tensors = lax.axis_size("tensor")
     factor = (inputs.shape[2] * tensors) ** (-0.5)
-    now, later = spread(inputs, tensors)
+    now, later = spread(inputs, tensors), inputs[1]
     half, velocity, debiased, grad = step(
         0, tensors, push_weight, numerators[0], swapped_all(now), cotangent, momentum[0], factor
     )

time: 130 us -> 130 us (level)
  local copies, waits for them, and re-layouts: 0.99 us -> 4.05 us
  Pallas kernels: 22.9 us -> 20.8 us
  starting transfers between devices: 19.6 us -> 18.1 us
    pallas_call x8, Pallas kernels: 22.9 us -> 20.8 us  [call(): pl.pallas_call(kernel, out_shape=out_shape, in_specs=in_specs or [VMEM] *...]
    ppermute x2, waiting for transfers between devices: 65.6 us -> 67.4 us  [passed_along(): return lax.ppermute(block, 'gossip', route)]
    all_to_all x3, waiting for transfers between devices: 18.6 us -> 17 us  [swapped_all(): return lax.all_to_all(blocks, 'tensor', 0, 0)]
    squeeze x0 -> x1, local copies, waits for them, and re-layouts: none -> 1.6 us  [body(): now, later = (spread(inputs, tensors), inputs[1])]
    all_to_all x3, starting transfers between devices: 13.9 us -> 12.4 us  [swapped_all(): return lax.all_to_all(blocks, 'tensor', 0, 0)]
    cond x6, local copies, waits for them, and re-layouts: 0.01 us -> 1.47 us
  transfers between devices with their start and end apart: 5 -> 5, of which waited for: 3 -> 3; matrix products, arithmetic and copies ran while one was open for 0% -> 1% of each run, Pallas kernels for 6% -> 6%
where the time goes in v1:
time: 130 us; the launch traced here: 129 us
  waiting for transfers between devices  84.4 us (65%)
  Pallas kernels  20.8 us (16%)
  starting transfers between devices  18.1 us (14%)
  local copies, waits for them, and re-layouts  4.05 us (3%)
  between operations  1.98 us (2%)
    ppermute x2, waiting for transfers between devices, passed_along(): return lax.ppermute(block, 'gossip', route)  67.4 us
    pallas_call x8, Pallas kernels, call(): pl.pallas_call(kernel, out_shape=out_shape, in_specs=in_specs or [VMEM] *...  20.8 us
    all_to_all x3, waiting for transfers between devices, swapped_all(): return lax.all_to_all(blocks, 'tensor', 0, 0)  17 us
    all_to_all x3, starting transfers between devices, swapped_all(): return lax.all_to_all(blocks, 'tensor', 0, 0)  12.4 us
    ppermute x2, starting transfers between devices, passed_along(): return lax.ppermute(block, 'gossip', route)  5.73 us
  transfers between devices with their start and end apart: 5, of which 3 were waited for; matrix products, arithmetic and copies ran while one was open for 1% of the time, Pallas kernels for 6%

profile of v1, /device:TPU:16, one launch (start us, length us, event | category | flops | bytes accessed | tf_op | source)
XLA Modules:
  0.0 129.4 jit_solution(10295655141686248586)
XLA Ops:
  0.6 0.0 copy-start.13
  0.6 1.0 copy-done.13
  1.6 1.3 %spread.1 = bf16[8,1,320,256]{3,2,1,0:T(8,128)(2,1)} custom-call(bf16[2,320,256]{2,1,0:T(8,128)(2,1)S(1)} %bitcast.16), custom_call_target="tpu_custom_call" | custom-call | bytes 1048576 | tf_op jit(solution)/shard_map/spread/pallas_call | solution.py:66
  3.0 0.0 copy-start.9
  3.0 0.0 copy-start.10
  3.0 5.2 %all-to-all-start.12 = ((bf16[8,1,320,256]{3,2,1,0:T(8,128)(2,1)}), bf16[8,1,320,256]{3,2,1,0:T(8,128)(2,1)S(1)}, u32[]{:S(2)}, u32[]{:S(2)}) async-start(bf16[8,1,320,256]{3,2,1,0:T(8,128)(2,1)} %spread.1), calls=%async_computation.12 | async-start | bytes 2621440 | tf_op jit(solution)/shard_map/all_to_all | solution.py:301
  9.5 1.6 %slice_bitcast_fusion = bf16[320,256]{1,0:T(8,128)(2,1)} fusion(bf16[2,320,256]{2,1,0:T(8,128)(2,1)} %bitcast.15), kind=kLoop, calls=%fused_computation | loop fusion | bytes 327680 | tf_op jit(solution)/shard_map/squeeze | solution.py:349
  11.0 17.0 %all-to-all-done.12.features = bf16[8,1,320,256]{3,2,1,0:T(8,128)(2,1)S(1)} async-done(((bf16[8,1,320,256]{3,2,1,0:T(8,128)(2,1)}), bf16[8,1,320,256]{3,2,1,0:T(8,128)(2,1)S(1)}, u32[]{:S(2)}, u32[]{:S(2)}) %all-to-all-start.12) | async-done | bytes 1310752 | tf_op jit(solution)/shard_map/all_to_all | solution.py:301
  28.1 0.0 copy-done.9
  28.1 0.0 copy-done.10
  28.1 4.9 %optimizer_step.13 = (bf16[2064,256]{1,0:T(8,128)(2,1)}, bf16[2048,256]{1,0:T(8,128)(2,1)}, bf16[2048,256]{1,0:T(8,128)(2,1)}, bf16[320,256]{1,0:T(8,128)(2,1)}) custom-call(f32[1]{0:T(128)S(6)} %copy.34.weight_ref, bf16[2048,256]{1,0:T(8,128)(2,1)S(1)} %bitcast.13, bf16[8,1,320,256]{3,2,1,0:T(8,128)(2,1)S(1)} %all-to-all-done.12.features, ...), custom_call_target="tpu_custom_call" | custom-call | flops 671088640 | bytes 8388608 | tf_op jit(solution)/shard_map/optimizer_step/pallas_call | solution.py:66
  33.0 0.0 copy-done.22
  33.0 96.4 %conditional.1 = (bf16[2048,256]{1,0:T(8,128)(2,1)}, bf16[2048,256]{1,0:T(8,128)(2,1)}, f32[1]{0:T(128)}, bf16[2,320,256]{2,1,0:T(8,128)(2,1)}) conditional(s32[]{:T(128)} %clamp.3, (bf16[2064,256]{1,0:T(8,128)(2,1)}, bf16[320,256]{1,0:T(8,128)(2,1)S(1)}, bf16[2,320,256]{2,1,0:T(8,128)(2,1)}, ...), branch_computations={%region_0.0_spmd, %region_1.0_spmd, %region_2.0_spmd, %region_3.0_... | conditional | flops 70061654016 | bytes 75334336 | solution.py:353
  33.0 3.8 %collective-permute-start.6 = (bf16[2064,256]{1,0:T(8,128)(2,1)}, bf16[2064,256]{1,0:T(8,128)(2,1)S(1)}, u32[]{:S(2)}, u32[]{:S(2)}) collective-permute-start(bf16[2064,256]{1,0:T(8,128)(2,1)} %get-tuple-element.110.own), channel_id=1, source_target_pairs={{0,32},{8,40},{16,48},{24,56},{32,64},{40,72},{48,80},{56,88},{64,... | collective-permute-start | bytes 3170312 | tf_op jit(solution)/shard_map/cond/branch_2_fun/ppermute | solution.py:37
  36.8 1.2 blocks_for_peers.14
  38.0 3.6 %all-to-all-start.4 = ((bf16[8,1,320,256]{3,2,1,0:T(8,128)(2,1)}), bf16[8,1,320,256]{3,2,1,0:T(8,128)(2,1)S(1)}, u32[]{:S(2)}, u32[]{:S(2)}) async-start(bf16[8,1,320,256]{3,2,1,0:T(8,128)(2,1)} %blocks_for_peers.14), calls=%async_computation.4 | async-start | bytes 2621440 | tf_op jit(solution)/shard_map/cond/branch_2_fun/all_to_all | solution.py:301
  41.6 25.4 %collective-permute-done.6.refs_0_ = bf16[2064,256]{1,0:T(8,128)(2,1)S(1)} collective-permute-done((bf16[2064,256]{1,0:T(8,128)(2,1)}, bf16[2064,256]{1,0:T(8,128)(2,1)S(1)}, u32[]{:S(2)}, u32[]{:S(2)}) %collective-permute-start.6) | collective-permute-done | bytes 1056800 | tf_op jit(solution)/shard_map/cond/branch_2_fun/ppermute | solution.py:37
  67.0 2.3 %average.16 = (bf16[2048,256]{1,0:T(8,128)(2,1)S(1)}, f32[1]{0:T(128)}) custom-call(bf16[2064,256]{1,0:T(8,128)(2,1)} %get-tuple-element.110.own, bf16[2064,256]{1,0:T(8,128)(2,1)S(1)} %collective-permute-done.6.refs_0_), custom_call_target="tpu_custom_call" | custom-call | flops 8589934592 | bytes 1048576 | tf_op jit(solution)/shard_map/cond/branch_2_fun/average/pallas_call | solution.py:66
  69.2 0.0 all-to-all-done.4.features
  69.2 0.0 copy-start.16
  69.3 0.0 copy-start.26
  69.3 5.6 %optimizer_step.9 = (bf16[2064,256]{1,0:T(8,128)(2,1)}, bf16[2048,256]{1,0:T(8,128)(2,1)}, bf16[2048,256]{1,0:T(8,128)(2,1)S(1)}, bf16[320,256]{1,0:T(8,128)(2,1)S(1)}) custom-call(f32[1]{0:T(128)} %get-tuple-element.111.weight_ref, bf16[2048,256]{1,0:T(8,128)(2,1)S(1)} %get-tuple-element.112.numer, bf16[8,1,320,256]{3,2,1,0:T(8,128)(2,1)S(1)} %all-to-all-done.4.features, ...), custom_call_target="tpu_custom_call" | custom-call | flops 671088640 | bytes 8388608 | tf_op jit(solution)/shard_map/cond/branch_2_fun/optimizer_step/pallas_call | solution.py:66
  74.9 1.9 %collective-permute-start.7 = (bf16[2064,256]{1,0:T(8,128)(2,1)}, bf16[2064,256]{1,0:T(8,128)(2,1)}, u32[]{:S(2)}, u32[]{:S(2)}) collective-permute-start(bf16[2064,256]{1,0:T(8,128)(2,1)} %get-tuple-element.118.own), channel_id=1, source_target_pairs={{0,64},{8,72},{16,80},{24,88},{32,96},{40,104},{48,112},{56,120},{... | collective-permute-start | bytes 3170312 | tf_op jit(solution)/shard_map/cond/branch_2_fun/ppermute | solution.py:37
  76.8 0.0 copy-done.16
  76.8 0.0 copy-done.26
  76.8 1.5 %blocks_for_peers.15 = bf16[8,2,320,256]{3,2,1,0:T(8,128)(2,1)S(1)} custom-call(bf16[2048,256]{1,0:T(8,128)(2,1)S(1)} %copy-done.16, bf16[320,256]{1,0:T(8,128)(2,1)S(1)} %copy-done.26, bf16[2048,256]{1,0:T(8,128)(2,1)S(1)} %get-tuple-element.116.refs_2_, bf16[320,256]{1,0:T(8,128)(2,1)S(1)} %get-tuple-element.117.refs_3_), custom_call_target="tpu_custom_call" | custom-call | flops 671088640 | bytes 3145728 | tf_op jit(solution)/shard_map/cond/branch_2_fun/blocks_for_peers/pallas_call | solution.py:66
  78.4 1.5 %copy-done.3 = bf16[8,2,320,256]{3,2,1,0:T(8,128)(2,1)} copy-done((bf16[8,2,320,256]{3,2,1,0:T(8,128)(2,1)}, bf16[8,2,320,256]{3,2,1,0:T(8,128)(2,1)S(1)}, u32[]{:S(2)}) %copy-start.3) | copy-done | bytes 2621464 | tf_op jit(solution)/shard_map/cond
  79.8 3.6 %all-to-all-start.5 = ((bf16[8,2,320,256]{3,2,1,0:T(8,128)(2,1)}), bf16[8,2,320,256]{3,2,1,0:T(8,128)(2,1)S(1)}, u32[]{:S(2)}, u32[]{:S(2)}) async-start(bf16[8,2,320,256]{3,2,1,0:T(8,128)(2,1)} %copy-done.3), calls=%async_computation.5 | async-start | bytes 5242880 | tf_op jit(solution)/shard_map/cond/branch_2_fun/all_to_all | solution.py:301
  83.4 42.0 %collective-permute-done.7.refs_0_ = bf16[2064,256]{1,0:T(8,128)(2,1)} collective-permute-done((bf16[2064,256]{1,0:T(8,128)(2,1)}, bf16[2064,256]{1,0:T(8,128)(2,1)}, u32[]{:S(2)}, u32[]{:S(2)}) %collective-permute-start.7) | collective-permute-done | bytes 1056800 | tf_op jit(solution)/shard_map/cond/branch_2_fun/ppermute | solution.py:37
  125.4 2.9 %average.17 = (bf16[2048,256]{1,0:T(8,128)(2,1)}, f32[1]{0:T(128)}) custom-call(bf16[2064,256]{1,0:T(8,128)(2,1)} %get-tuple-element.118.own, bf16[2064,256]{1,0:T(8,128)(2,1)} %collective-permute-done.7.refs_0_), custom_call_target="tpu_custom_call" | custom-call | flops 34359738368 | bytes 1048576 | tf_op jit(solution)/shard_map/cond/branch_2_fun/average/pallas_call | solution.py:66
  128.4 0.0 all-to-all-done.5.first_ref.second_ref
  128.4 1.1 collect.6
  (2 shorter events, 0.0 us)
Async XLA Ops:
  0.6 1.0 copy-start.13
  3.0 25.1 %copy-start.9 = (bf16[1,2048,256]{2,1,0:T(8,128)(2,1)S(1)}, bf16[1,2048,256]{2,1,0:T(8,128)(2,1)}, u32[]{:S(2)}) copy-start(bf16[1,2048,256]{2,1,0:T(8,128)(2,1)} %param.14) | copy-start | bytes 3145732
  3.0 25.1 %copy-start.10 = (bf16[1,2048,256]{2,1,0:T(8,128)(2,1)S(1)}, bf16[1,2048,256]{2,1,0:T(8,128)(2,1)}, u32[]{:S(2)}) copy-start(bf16[1,2048,256]{2,1,0:T(8,128)(2,1)} %param.15) | copy-start | bytes 3145732
  3.0 25.1 %all-to-all-start.12 = ((bf16[8,1,320,256]{3,2,1,0:T(8,128)(2,1)}), bf16[8,1,320,256]{3,2,1,0:T(8,128)(2,1)S(1)}, u32[]{:S(2)}, u32[]{:S(2)}) async-start(bf16[8,1,320,256]{3,2,1,0:T(8,128)(2,1)} %spread.1), calls=%async_computation.12 | async-start | bytes 2621440 | tf_op jit(solution)/shard_map/all_to_all | solution.py:301
  28.1 4.9 %copy-start.22 = (bf16[320,256]{1,0:T(8,128)(2,1)S(1)}, bf16[320,256]{1,0:T(8,128)(2,1)}, u32[]{:S(2)}) copy-start(bf16[320,256]{1,0:T(8,128)(2,1)} %slice_bitcast_fusion) | copy-start | bytes 491524
  33.0 34.0 %collective-permute-start.6 = (bf16[2064,256]{1,0:T(8,128)(2,1)}, bf16[2064,256]{1,0:T(8,128)(2,1)S(1)}, u32[]{:S(2)}, u32[]{:S(2)}) collective-permute-start(bf16[2064,256]{1,0:T(8,128)(2,1)} %get-tuple-element.110.own), channel_id=1, source_target_pairs={{0,32},{8,40},{16,48},{24,56},{32,64},{40,72},{48,80},{56,88},{64,... | collective-permute-start | bytes 3170312 | tf_op jit(solution)/shard_map/cond/branch_2_fun/ppermute | solution.py:37
  38.0 31.3 %all-to-all-start.4 = ((bf16[8,1,320,256]{3,2,1,0:T(8,128)(2,1)}), bf16[8,1,320,256]{3,2,1,0:T(8,128)(2,1)S(1)}, u32[]{:S(2)}, u32[]{:S(2)}) async-start(bf16[8,1,320,256]{3,2,1,0:T(8,128)(2,1)} %blocks_for_peers.14), calls=%async_computation.4 | async-start | bytes 2621440 | tf_op jit(solution)/shard_map/cond/branch_2_fun/all_to_all | solution.py:301
  69.2 7.6 %copy-start.16 = (bf16[2048,256]{1,0:T(8,128)(2,1)S(1)}, bf16[2048,256]{1,0:T(8,128)(2,1)}, u32[]{:S(2)}) copy-start(bf16[2048,256]{1,0:T(8,128)(2,1)} %get-tuple-element.108.refs_0_) | copy-start | bytes 3145732 | tf_op jit(solution)/shard_map/cond
  69.3 7.6 %copy-start.26 = (bf16[320,256]{1,0:T(8,128)(2,1)S(1)}, bf16[320,256]{1,0:T(8,128)(2,1)}, u32[]{:S(2)}) copy-start(bf16[320,256]{1,0:T(8,128)(2,1)} %get-tuple-element.109.refs_1_) | copy-start | bytes 491524 | tf_op jit(solution)/shard_map/cond
  74.9 50.5 %collective-permute-start.7 = (bf16[2064,256]{1,0:T(8,128)(2,1)}, bf16[2064,256]{1,0:T(8,128)(2,1)}, u32[]{:S(2)}, u32[]{:S(2)}) collective-permute-start(bf16[2064,256]{1,0:T(8,128)(2,1)} %get-tuple-element.118.own), channel_id=1, source_target_pairs={{0,64},{8,72},{16,80},{24,88},{32,96},{40,104},{48,112},{56,120},{... | collective-permute-start | bytes 3170312 | tf_op jit(solution)/shard_map/cond/branch_2_fun/ppermute | solution.py:37
  78.3 1.5 %copy-start.3 = (bf16[8,2,320,256]{3,2,1,0:T(8,128)(2,1)}, bf16[8,2,320,256]{3,2,1,0:T(8,128)(2,1)S(1)}, u32[]{:S(2)}) copy-start(bf16[8,2,320,256]{3,2,1,0:T(8,128)(2,1)S(1)} %blocks_for_peers.15) | copy-start | bytes 7864324 | tf_op jit(solution)/shard_map/cond
  79.8 48.5 %all-to-all-start.5 = ((bf16[8,2,320,256]{3,2,1,0:T(8,128)(2,1)}), bf16[8,2,320,256]{3,2,1,0:T(8,128)(2,1)S(1)}, u32[]{:S(2)}, u32[]{:S(2)}) async-start(bf16[8,2,320,256]{3,2,1,0:T(8,128)(2,1)} %copy-done.3), calls=%async_computation.5 | async-start | bytes 5242880 | tf_op jit(solution)/shard_map/cond/branch_2_fun/all_to_all | solution.py:301
